TPU v7x, 512 devices: a whole 4x8x8 slice. The times are simulated.
512 devices in a mesh: group: 16 (over z_hi, y), tensor: 8 (over x, core), blk: 4 (over z_lo).
Axes of the slice: x: 4, y: 8, z: 8 (z_hi: 2, z_lo: 4; z = z_hi * 4 + z_lo), core: 2. Of those that a mesh axis runs over, the one named last changes fastest.
Arguments:
- trainer_input_rows: bfloat16 [2048, 5120], P('group', 'blk'), may hold values from -6 to 6
- policy_output_cotangent: bfloat16 [2048, 8192], P('group', 'tensor'), may hold values from -6 to 6
- down_factor: float32 [5120, 64], P('blk'), may hold values from -0.078125 to 0.078125
- up_factor: float32 [64, 8192], P(None, 'tensor'), may hold values from -0.3125 to 0.3125
- frozen_query_weight: bfloat16 [5120, 8192], P('blk', 'tensor'), may hold values from -0.078125 to 0.078125
- decode_hidden_state: bfloat16 [512, 5120], P('group', 'blk'), may hold values from -6 to 6
- cached_key_block: bfloat16 [512, 128, 1024], P(('group', 'blk'), None, 'tensor'), may hold values from -1000 to 1000, as said below
- cached_value_block: bfloat16 [512, 128, 1024], P(('group', 'blk'), None, 'tensor'), may hold values from -6 to 6
- incoming_key: bfloat16 [512, 1024], P(('group', 'blk'), 'tensor'), may hold values from -6 to 6
- incoming_value: bfloat16 [512, 1024], P(('group', 'blk'), 'tensor'), may hold values from -6 to 6
- cache_live_length: int32 [512], P(('group', 'blk')), may hold values from 1 to 128
Outputs:
- updated_down_factor: float32 [5120, 64], P('blk')
- updated_up_factor: float32 [64, 8192], P(None, 'tensor')
- attended: bfloat16 [512, 8192], P(('group', 'blk'), 'tensor')
Inputs may be any that keep to these rules, and one draw needn't show every extreme that they name: `cached_key_block`: finite keys.
All inputs are finite; a program needn't handle non-finite values.
Results may differ from a plain program's by a relative error of at most 0.013.
Values sent between devices are 32-bit elements; how exact they have to be, the bound alone decides.
A program may use at most 64 MiB of HBM per device.

v0:
```python
import math

import jax
import jax.numpy as jnp
from jax import lax
from jax.sharding import PartitionSpec as P

HEAD_SIZE = 128


adapter_scale = 2.0
learning_rate = 0.1
highest_precision = lax.Precision.HIGHEST


def attend_local(query, keys, values, own_key, own_value, lengths):
    count = query.shape[0]
    kv_heads = own_key.shape[1] // HEAD_SIZE
    span = keys.shape[1]
    adapter_factor = 1.0 / math.sqrt(HEAD_SIZE)
    query_heads = query.reshape(count, kv_heads, -1, HEAD_SIZE)
    key_heads = keys.reshape(count, span, kv_heads, HEAD_SIZE)
    value_heads = values.reshape(count, span, kv_heads, HEAD_SIZE)
    own_k = own_key.reshape(count, kv_heads, HEAD_SIZE)
    own_v = own_value.astype(jnp.float32).reshape(count, kv_heads, HEAD_SIZE)
    scores = (
        jnp.einsum("nkgd,nlkd->nkgl", query_heads, key_heads, preferred_element_type=jnp.float32)
        * adapter_factor
    )
    live = (jnp.arange(span)[None, :] < lengths[:, None])[:, None, None, :]
    scores = jnp.where(live, scores, -1e30)
    own_score = (
        jnp.einsum("nkgd,nkd->nkg", query_heads, own_k, preferred_element_type=jnp.float32)
        * adapter_factor
    )
    peak = jnp.maximum(jnp.max(scores, axis=-1), own_score)
    expo = jnp.where(live, jnp.exp(scores - peak[..., None]), 0.0)
    own_expo = jnp.exp(own_score - peak)
    total = jnp.sum(expo, axis=-1) + own_expo
    weights = (expo / total[..., None]).astype(jnp.bfloat16)
    own_weight = (own_expo / total).astype(jnp.bfloat16)
    mixed = jnp.einsum("nkgl,nlkd->nkgd", weights, value_heads, preferred_element_type=jnp.float32)
    mixed = mixed + own_weight.astype(jnp.float32)[..., None] * own_v[:, :, None, :]
    return mixed.reshape(count, -1).astype(jnp.bfloat16)


def local(
    trainer_input_rows,
    policy_output_cotangent,
    down_factor,
    up_factor,
    frozen_query_weight,
    decode_hidden_state,
    cached_key_block,
    cached_value_block,
    incoming_key,
    incoming_value,
    cache_live_length,
):
    input_rows_flat = trainer_input_rows.astype(jnp.float32)
    cotangent_rows = policy_output_cotangent.astype(jnp.float32)
    rank_product = lax.psum(
        jnp.dot(input_rows_flat, down_factor, precision=highest_precision), "blk"
    )
    backward_projection = lax.psum(
        jnp.dot(cotangent_rows, up_factor.T, precision=highest_precision), "tensor"
    )
    part_a = jnp.dot(input_rows_flat.T, backward_projection, precision=highest_precision)
    part_b = jnp.dot(rank_product.T, cotangent_rows, precision=highest_precision)
    adapter_factor = adapter_scale / (trainer_input_rows.shape[0] * lax.axis_size("group"))
    group_down_gradient, group_up_gradient = lax.psum((part_a, part_b), "group")
    updated_down_factor = down_factor - learning_rate * (group_down_gradient * adapter_factor)
    updated_up_factor = up_factor - learning_rate * (group_up_gradient * adapter_factor)
    merged = frozen_query_weight.astype(jnp.float32) + adapter_scale * jnp.dot(
        updated_down_factor, updated_up_factor, precision=highest_precision
    )
    hidden_rows = decode_hidden_state.astype(jnp.float32)
    query = lax.psum_scatter(
        jnp.dot(hidden_rows, merged, precision=highest_precision),
        "blk",
        scatter_dimension=0,
        tiled=True,
    ).astype(jnp.bfloat16)
    attended = attend_local(
        query, cached_key_block, cached_value_block, incoming_key, incoming_value, cache_live_length
    )
    return (updated_down_factor, updated_up_factor, attended)


def solution(mesh):
    return jax.shard_map(
        local,
        mesh=mesh,
        in_specs=(
            P("group", "blk"),
            P("group", "tensor"),
            P("blk", None),
            P(None, "tensor"),
            P("blk", "tensor"),
            P("group", "blk"),
            P(("group", "blk"), None, "tensor"),
            P(("group", "blk"), None, "tensor"),
            P(("group", "blk"), "tensor"),
            P(("group", "blk"), "tensor"),
            P(("group", "blk")),
        ),
        out_specs=(P("blk", None), P(None, "tensor"), P(("group", "blk"), "tensor")),
        check_vma=False,
    )
```

profile of v0, /device:TPU:1, one launch (start us, length us, event | category | flops | bytes accessed | tf_op | source)
XLA Modules:
  0.0 301.3 jit_solution(13175813134957487786)
XLA Ops:
  7.2 0.0 copy-start
  7.2 0.0 all-reduce.3.cloned.1.call-start
  7.2 1.4 fusion.25
  8.7 0.0 copy-start.1
  8.7 27.9 %psum.28 = f32[128,64]{1,0:T(8,128)S(1)} all-reduce(f32[128,64]{1,0:T(8,128)S(1)} %fusion.25), channel_id=1, replica_groups=mesh['group'=16,'tensor'=8,'blk'=4] {'tensor'}, use_global_device_ids=true, to_apply=%region_0.0 | all-reduce | flops 8192 | bytes 65536 | tf_op jit(solution)/shard_map/psum | solution.py:65
  36.6 1.1 convolution_bitcast_fusion
  37.7 1.4 fusion.26
  39.1 14.9 %psum.30 = f32[128,64]{1,0:T(8,128)S(1)} all-reduce(f32[128,64]{1,0:T(8,128)S(1)} %fusion.26), channel_id=1, replica_groups=mesh['group'=16,'tensor'=8,'blk'=4] {'blk'}, use_global_device_ids=true, to_apply=%region_2.0 | all-reduce | flops 8192 | bytes 65536 | tf_op jit(solution)/shard_map/psum | solution.py:62
  54.0 2.0 fusion.27
  56.0 0.0 all-reduce.3.cloned.1.call-update
  56.0 0.0 reduce-scatter.2.cloned.1.call-start
  56.0 192.9 %all-reduce.3.cloned.1.call-done = (f32[1280,64]{0,1:T(8,128)}, f32[64,1024]{1,0:T(8,128)}) async-done(((f32[1280,64]{0,1:T(8,128)}, f32[64,1024]{1,0:T(8,128)}), (f32[1280,64]{0,1:T(8,128)}, f32[64,1024]{1,0:T(8,128)})) %all-reduce.3.cloned.1.call-update) | async-done | bytes 589840 | tf_op jit(solution)/shard_map/psum | solution.py:71
  248.9 1.1 multiply_subtract_fusion
  250.0 0.0 copy-start.2
  250.0 1.2 multiply_subtract_fusion.1
  251.2 0.0 copy-start.3
  251.2 4.4 %fusion.28 = f32[1280,1024]{1,0:T(8,128)S(1)} fusion(f32[1280,64]{0,1:T(8,128)S(1)} %multiply_subtract_fusion, f32[64,1024]{1,0:T(8,128)S(1)} %multiply_subtract_fusion.1), kind=kOutput, calls=%fused_computation.39 | convolution fusion | flops 1006632960 | bytes 5832704 | tf_op jit(solution)/shard_map/dot_general | solution.py:74
  255.6 0.0 copy-done.1
  255.6 0.0 copy-start.4
  255.6 0.0 copy-start.6
  255.6 0.0 copy-start.5
  255.7 4.0 %fusion.5 = f32[32,1024]{1,0:T(8,128)} fusion(bf16[32,1280]{1,0:T(8,128)(2,1)} %param.16, f32[1280,1024]{1,0:T(8,128)S(1)} %fusion.28, bf16[1280,1024]{1,0:T(8,128)(2,1)S(1)} %copy-done.1), kind=kOutput, calls=%fused_computation.6 | convolution fusion | flops 507248640 | bytes 8077312 | tf_op jit(solution)/shard_map/dot_general | solution.py:79
  259.7 0.0 copy-done.2
  259.7 0.0 reduce-scatter.2.cloned.1.call-update
  259.7 0.1 iota_compare_fusion
  259.8 30.5 %reduce-scatter.2.cloned.1.call-done = f32[8,1024]{1,0:T(8,128)} async-done(((f32[32,1024]{1,0:T(8,128)}), f32[8,1024]{1,0:T(8,128)}) %reduce-scatter.2.cloned.1.call-update) | async-done | bytes 32784 | tf_op jit(solution)/shard_map/reduce_scatter | solution.py:78
  290.3 0.8 convert_bitcast_fusion
  291.1 0.1 fusion.16
  291.2 1.2 fusion.24
  292.5 0.2 fusion.11
  292.7 1.2 fusion.10
  293.9 0.6 copy.27
  (8 shorter events, 0.0 us)
Async XLA Ops:
  7.2 29.4 %copy-start = (bf16[128,1280]{1,0:T(8,128)(2,1)S(1)}, bf16[128,1280]{1,0:T(8,128)(2,1)}, u32[]{:S(2)}) copy-start(bf16[128,1280]{1,0:T(8,128)(2,1)} %param.11) | copy-start | bytes 983044
  7.2 241.7 %all-reduce.3.cloned.1.call-start = ((), (), s32[]{:S(2)}) async-start(), calls=%async_computation.2 | async-start | bytes 1179648 | tf_op jit(solution)/shard_map/psum | solution.py:71
  8.7 246.9 %copy-start.1 = (bf16[1280,1024]{1,0:T(8,128)(2,1)S(1)}, bf16[1280,1024]{1,0:T(8,128)(2,1)}, u32[]{:S(2)}) copy-start(bf16[1280,1024]{1,0:T(8,128)(2,1)} %param.15) | copy-start | bytes 7864324
  56.0 234.3 %reduce-scatter.2.cloned.1.call-start = ((), (), s32[]{:S(2)}) async-start(), calls=%async_computation.1 | async-start | bytes 163840 | tf_op jit(solution)/shard_map/reduce_scatter | solution.py:78
  250.0 9.7 %copy-start.2 = (f32[1280,64]{0,1:T(8,128)}, f32[1280,64]{0,1:T(8,128)S(1)}, u32[]{:S(2)}) copy-start(f32[1280,64]{0,1:T(8,128)S(1)} %multiply_subtract_fusion) | copy-start | bytes 983044
  251.2 8.5 %copy-start.3 = (f32[64,1024]{1,0:T(8,128)}, f32[64,1024]{1,0:T(8,128)S(1)}, u32[]{:S(2)}) copy-start(f32[64,1024]{1,0:T(8,128)S(1)} %multiply_subtract_fusion.1) | copy-start | bytes 786436
  255.6 4.1 %copy-start.4 = (bf16[8,128]{1,0:T(8,128)(2,1)S(1)}, bf16[8,128]{1,0:T(8,128)(2,1)}, u32[]{:S(2)}) copy-start(bf16[8,128]{1,0:T(8,128)(2,1)} %param.20) | copy-start | bytes 6148
  255.6 4.1 %copy-start.6 = (s32[8]{0:T(128)S(1)}, s32[8]{0:T(128)}, u32[]{:S(2)}) copy-start(s32[8]{0:T(128)} %param.21) | copy-start | bytes 100
  255.6 35.4 %copy-start.5 = (bf16[8,128]{1,0:T(8,128)(2,1)S(1)}, bf16[8,128]{1,0:T(8,128)(2,1)}, u32[]{:S(2)}) copy-start(bf16[8,128]{1,0:T(8,128)(2,1)} %param.19) | copy-start | bytes 6148
Sparse Core Ops, SparseCore 0:
  56.1 192.7 all-reduce.2
  259.8 30.4 reduce-scatter.1
where the time goes:
time: 303 us; the launch traced here: 301 us
  waiting for transfers between devices  223 us (74%)
  blocking collectives  42.8 us (14%)
  matrix products  16.8 us (6%)
  between operations  14.2 us (5%)
  other arithmetic  3.35 us (1%)
    psum x1, waiting for transfers between devices, local(): group_down_gradient, group_up_gradient = lax.psum((part_a, part_b), 'group')  193 us
    reduce_scatter x1, waiting for transfers between devices, local(): lax.psum_scatter(jnp.dot(hidden_rows, merged, precision=highest_precision...  30.5 us
    psum x1, blocking collectives, local(): lax.psum(jnp.dot(cotangent_rows, up_factor.T, precision=highest_precision...  27.9 us
    psum x1, blocking collectives, local(): lax.psum(jnp.dot(input_rows_flat, down_factor, precision=highest_precisio...  14.9 us
  transfers between devices with their start and end apart: 2, of which 2 were waited for; matrix products, arithmetic and copies ran while one was open for 0% of the time, Pallas kernels for 0%

commit v1 on v0

v1 whole, which is shorter than its diff:
```python
import math

import jax
import jax.numpy as jnp
from jax import lax
from jax.experimental import pallas as pl
from jax.experimental.pallas import tpu as pltpu
from jax.sharding import PartitionSpec as P

MESH = pl.DeviceIdType.MESH
f32, bf16 = jnp.float32, jnp.bfloat16

adapter_scale = 2.0
learning_rate = 0.1
TOKENS = 2048
STEP = learning_rate * adapter_scale / TOKENS
OWNERS = 5
FAR_FIRST = (4, 5, 3, 7, 6, 2, 1)


def split(v):
    hi = v.astype(bf16)
    return hi, (v - hi.astype(f32)).astype(bf16)


def dot_nt(p, q):
    return lax.dot_general(p, q, (((1,), (1,)), ((), ())), preferred_element_type=f32)


def dot_nn(p, q):
    return jnp.dot(p, q, preferred_element_type=f32)


def twice(dot, v, q):
    rows = v.shape[0]
    hi, lo = split(v)
    both = dot(jnp.concatenate([hi, lo], axis=0), q)
    return both[:rows] + both[rows:]


def exchange(
    x_any, c_any, at_any, b_any, w_any, h_any, k_any, v_any, ik_any, iv_any, len_any,
    at_out, b_out, att_out,
    x, c, at, bu, w, hid, kc, vc, ik, iv, lens,
    p_part, p_recv, a_part, a1_recv, a_half, a2_send, a2_recv, a_full,
    b_part, b1_recv, b_line, b_full,
    hw_part, hw_recv, hx_send, hx_recv, u_send, u_all, fold,
    in_sem, p_s, p_r, a1_s, a1_r, a2_s, a2_r, a3_s, a3_r, a4_s, a4_r, a5_s, a5_r,
    b1_s, b1_r, b2_s, b2_r, b3_s, b3_r, hw_s, hw_r, hx_s, hx_r, u_s, u_r,
):
    g, t, b = lax.axis_index("group"), lax.axis_index("tensor"), lax.axis_index("blk")
    zh, y = lax.div(g, 8), lax.rem(g, 8)
    core = lax.rem(t, 2)
    z = zh * 4 + b
    y_first = core == 0
    m, n = jnp.where(y_first, y, z), jnp.where(y_first, z, y)

    def at_yt(dy, dt):
        return (zh * 8 + (y ^ dy), t ^ dt, b)

    def at_zt(dz, dt):
        far = z ^ dz
        return (lax.div(far, 4) * 8 + y, t ^ dt, lax.rem(far, 4))

    def at_y(d):
        return at_yt(d, 0)

    def at_z(d):
        return at_zt(d, 0)

    def at_t(d):
        return (g, t ^ d, b)

    def first(d):
        return tuple(jnp.where(y_first, p, q) for p, q in zip(at_y(d), at_z(d)))

    def second(d):
        return tuple(jnp.where(y_first, q, p) for p, q in zip(at_y(d), at_z(d)))

    barrier = pltpu.get_barrier_semaphore()
    for d in FAR_FIRST:
        for device in (at_t(d), at_y(d), at_z(d)):
            pl.semaphore_signal(barrier, inc=1, device_id=device, device_id_type=MESH)

    loads = [
        pltpu.make_async_copy(src, dst, in_sem.at[i])
        for i, (src, dst) in enumerate(
            zip(
                (c_any, b_any, x_any, at_any, h_any, w_any, k_any, v_any, ik_any, iv_any, len_any),
                (c, bu, x, at, hid, w, kc, vc, ik, iv, lens),
            )
        )
    ]
    for copy in loads:
        copy.start()

    arrivals, departures = {}, []

    def send(name, src, dst, sems, i, device):
        copy = pltpu.make_async_remote_copy(
            src_ref=src, dst_ref=dst, send_sem=sems[0].at[i], recv_sem=sems[1].at[i],
            device_id=device, device_id_type=MESH,
        )
        copy.start()
        arrivals.setdefault(name, []).append(copy.wait_recv)
        departures.append(copy.wait_send)

    def send_if(name, out, src, come, dst, sems, i, device):
        copy = pltpu.make_async_remote_copy(
            src_ref=src, dst_ref=dst, send_sem=sems[0].at[i], recv_sem=sems[1].at[i],
            device_id=device, device_id_type=MESH,
        )
        pl.when(out)(copy.start)
        arrivals.setdefault(name, []).append(lambda: pl.when(come)(copy.wait_recv))
        departures.append(lambda: pl.when(out)(copy.wait_send))

    def arrive(name):
        for wait in arrivals.pop(name):
            wait()

    def rows(d):
        return pl.ds(pl.multiple_of(d * 8, 8), 8)

    def hidden_chunk(i):
        cols = pl.ds(i * 256, 256)
        hw_part[:, :, cols] = dot_nn(hid[...], w[:, cols]).reshape(4, 8, 256)

    loads[0].wait()
    loads[1].wait()
    p_part[...] = twice(dot_nt, bu[...], c[...]).reshape(8, 8, 128)

    loads[2].wait()
    loads[3].wait()
    low = twice(dot_nt, at[...], x[...])
    grad_b = twice(dot_nn, low, c[...])
    for i in range(8):
        for j in range(8):
            place = jnp.where(y_first, j * 8 + i, i * 8 + j)
            b_part[pl.ds(place, 1)] = grad_b[i * 8 : i * 8 + 8, j * 128 : j * 128 + 128].reshape(1, 8, 128)
    loads[4].wait()
    hx_send[...] = hid[...].astype(f32).reshape(8, 4, 1280)

    pl.semaphore_wait(barrier, 21)
    for d in FAR_FIRST:
        send("p", p_part.at[t ^ d], p_recv.at[d - 1], (p_s, p_r), d - 1, at_t(d))
    for d in FAR_FIRST:
        send("b1", b_part.at[rows(m ^ d)], b1_recv.at[d - 1], (b1_s, b1_r), d - 1, first(d))

    send("hx", hx_send.at[t], hx_recv.at[t], (hx_s, hx_r), 0, at_z(4))

    into = lax.broadcasted_iota(jnp.int32, (1024, 64), 0)
    out = lax.broadcasted_iota(jnp.int32, (1024, 64), 1)
    hit = (lax.div(into, 128) == lax.div(out, 8)) & (lax.rem(into, 8) == lax.rem(out, 8))
    fold[...] = jnp.where(hit, 1.0, 0.0).astype(bf16)

    loads[5].wait()
    hidden_chunk(0)
    hidden_chunk(1)

    arrive("p")
    back = p_part[t]
    for d in range(7):
        back = back + p_recv[d]
    grad_a = twice(dot_nn, back, x[...])
    for i in range(OWNERS):
        a_part[i] = grad_a[:, i * 256 : i * 256 + 256]
    owner = y < OWNERS
    piece = jnp.minimum(y, OWNERS - 1)
    for d in FAR_FIRST:
        send_if("a1", (y ^ d) < OWNERS, a_part.at[jnp.minimum(y ^ d, OWNERS - 1)], owner, a1_recv.at[d - 1], (a1_s, a1_r), d - 1, at_y(d))
    hidden_chunk(2)
    hidden_chunk(3)

    old = at[rows(t), pl.ds(pl.multiple_of(piece * 256, 256), 256)]

    @pl.when(owner)
    def _():
        for wait in arrivals["a1"]:
            wait()
        total = a_part[piece]
        for d in range(7):
            total = total + a1_recv[d]
        a2_send[...] = total
        a_half[piece] = jnp.where(zh == 0, old, 0.0) - STEP * total

    arrivals.pop("a1")
    for d in FAR_FIRST:
        send_if("a3", owner, a_half.at[piece], (y ^ d) < OWNERS, a_half.at[piece], (a3_s, a3_r), d - 1, at_y(d))
    send_if("a2", owner, a2_send, owner, a2_recv, (a2_s, a2_r), 0, at_z(4))
    arrive("hx")
    for d in FAR_FIRST:
        send("hx2", hx_recv.at[t], hx_recv.at[t], (hx_s, hx_r), d, at_t(d))

    arrive("b1")
    total = b_part[rows(m)]
    for d in range(7):
        total = total + b1_recv[d]
    b_line[n] = total
    for d in FAR_FIRST:
        send("b2", b_line.at[n], b_line.at[n], (b2_s, b2_r), d - 1, second(d))
    for d in (3, 2, 1):
        send("hw", hw_part.at[b ^ d], hw_recv.at[d - 1], (hw_s, hw_r), d - 1, at_z(d))

    @pl.when(owner)
    def _():
        for wait in arrivals["a2"]:
            wait()
        a_full[t, piece] = old - STEP * (a2_send[...] + a2_recv[...])

    arrivals.pop("a2")
    for i, dt in enumerate((4, 2, 6, 0)):
        for d in FAR_FIRST + (0,):
            if d or dt:
                send_if(
                    "a4" + str(dt), owner, a_full.at[t, piece], (y ^ d) < OWNERS, a_full.at[t, piece], (a4_s, a4_r), i * 8 + d, at_yt(d, dt)
                )

    arrive("a3")
    arrive("hx2")
    near = jnp.zeros((64, 128), f32)
    both = jnp.concatenate([hid[...], hx_recv[...].reshape(32, 1280).astype(bf16)], axis=0)
    for i in range(OWNERS):
        hi, lo = split(jnp.concatenate([a_half[i]] * 8, axis=0))
        near = near + dot_nt(both[:, i * 256 : i * 256 + 256], jnp.concatenate([hi, lo], axis=0))
    lane = lax.broadcasted_iota(jnp.int32, (64, 128), 1)
    row = lax.broadcasted_iota(jnp.int32, (64, 128), 0)
    near = jnp.where(lax.rem(lax.div(lane, 8), 8) == lax.rem(row, 8), near, 0.0).reshape(2, 4, 8, 128)
    near = jnp.sum(near, axis=2, keepdims=True)
    u_send[pl.ds(zh * 4, 4)] = near[0]
    u_send[pl.ds(4 - zh * 4, 4)] = near[1]
    u_all[t * 8 + z] = u_send[z]
    for dz in (4, 5, 3, 7, 6, 2, 1, 0):
        for dt in (4, 5, 2, 3, 6, 7, 1, 0):
            if dz or dt:
                copy = pltpu.make_async_remote_copy(
                    src_ref=u_send.at[z ^ dz], dst_ref=u_all.at[t * 8 + z], send_sem=u_s, recv_sem=u_r,
                    device_id=at_zt(dz, dt), device_id_type=MESH,
                )
                copy.start()

    arrive("b2")
    total = b_line[0]
    for i in range(1, 8):
        total = total + b_line[i]
    for i in range(8):
        line, col = jnp.where(y_first, i, m), jnp.where(y_first, m, i)
        tile = bu[rows(line), pl.ds(pl.multiple_of(col * 128, 128), 128)]
        b_full[m, i] = tile - STEP * total[i]
    for d in FAR_FIRST:
        send("b3", b_full.at[m], b_full.at[m], (b3_s, b3_r), d - 1, first(d))

    arrive("hw")
    base = hw_part[b]
    for d in range(3):
        base = base + hw_recv[d]

    for i, dt in enumerate((0, 6, 2, 4)):
        arrive("a4" + str(dt))
        send("a5", a_full.at[t ^ dt], a_full.at[t ^ dt], (a5_s, a5_r), i, at_t(1))

    most = u_all.at[pl.ds(0, 63)]
    pltpu.make_async_copy(most, most, u_r).wait()
    slices = jnp.sum(u_all[...].reshape(8, 8, 1, 128), axis=1)
    lane = lax.broadcasted_iota(jnp.int32, (8, 128), 1)
    row = lax.broadcasted_iota(jnp.int32, (8, 128), 0)
    wide = jnp.concatenate(
        [jnp.where(lax.rem(lax.div(lane, 8), 8) == row, jnp.broadcast_to(slices[i], (8, 128)), 0.0) for i in range(8)], axis=1
    )
    hidden_low = twice(dot_nn, wide, fold[...])

    arrive("b3")
    for i in range(8):
        for j in range(8):
            first_at, second_at = jnp.where(y_first, j, i), jnp.where(y_first, i, j)
            b_out[i * 8 : i * 8 + 8, j * 128 : j * 128 + 128] = b_full[first_at, second_at]

    b_hi, b_lo = split(b_out[...])
    hi, lo = split(hidden_low)
    both = dot_nn(jnp.concatenate([hi, lo], axis=0), b_hi)
    query = base + adapter_scale * (both[:8] + both[8:] + dot_nn(hi, b_lo))

    for copy in loads[6:]:
        copy.wait()
    heads = jnp.concatenate([query[:, i * 128 : i * 128 + 128] for i in range(8)], axis=0).astype(bf16)
    scale = 1.0 / math.sqrt(128)
    scores = (dot_nt(heads, kc[...]) * scale).reshape(8, 8, 1024)
    row = lax.broadcasted_iota(jnp.int32, (8, 128), 0)
    slot = lax.broadcasted_iota(jnp.int32, (8, 128), 1)
    live = jnp.concatenate(
        [jnp.where((row == i) & (slot < lens[i]), 1.0, 0.0) for i in range(8)], axis=1
    )[None]
    live = jnp.broadcast_to(live, scores.shape) > 0.5
    scores = jnp.where(live, scores, -1e30)
    own_k = ik[...].astype(f32)[None]
    own = jnp.sum(heads.astype(f32).reshape(8, 8, 128) * own_k, axis=-1, keepdims=True) * scale
    peak = jnp.maximum(jnp.max(scores, axis=-1, keepdims=True), own)
    expo = jnp.where(live, jnp.exp(scores - peak), 0.0)
    own_expo = jnp.exp(own - peak)
    total = jnp.sum(expo, axis=-1, keepdims=True) + own_expo
    weights = (expo / total).astype(bf16).reshape(64, 1024)
    own_weight = (own_expo / total).astype(bf16).astype(f32)
    mixed = dot_nn(weights, vc[...]).reshape(8, 8, 128) + own_weight * iv[...].astype(f32)[None]
    mixed = mixed.astype(bf16)
    for i in range(8):
        att_out[:, i * 128 : i * 128 + 128] = mixed[i]

    arrive("a5")
    for i in range(8):
        for j in range(OWNERS):
            at_out[i * 8 : i * 8 + 8, j * 256 : j * 256 + 256] = a_full[i, j]

    for wait in departures:
        wait()
    pltpu.make_async_copy(most, most, u_s).wait()


def finish(at_in, b_in, att_in, at_out, b_out, att_out, sem):
    stores = [
        pltpu.make_async_copy(src, dst, sem.at[i])
        for i, (src, dst) in enumerate(((at_in, at_out), (b_in, b_out), (att_in, att_out)))
    ]
    for copy in stores:
        copy.start()
    for copy in stores:
        copy.wait()


def local(x, c, a, bu, w, hid, keys, values, ik, iv, lens):
    vm, dma = pltpu.VMEM, pltpu.SemaphoreType.DMA
    slots = keys.shape[0] * keys.shape[1]
    hbm = pl.BlockSpec(memory_space=pltpu.HBM)
    vmem = pl.BlockSpec(memory_space=pltpu.VMEM)

    def two(i):
        return [dma((i,)), dma((i,))]

    outs = (
        jax.ShapeDtypeStruct((64, 1280), f32),
        jax.ShapeDtypeStruct((64, 1024), f32),
        jax.ShapeDtypeStruct((8, 1024), bf16),
    )
    arrays = (x, c, a.T, bu, w, hid, keys.reshape(slots, 128), values.reshape(slots, 128), ik, iv, lens)
    new = pl.pallas_call(
        exchange,
        out_shape=outs,
        in_specs=[hbm] * 11,
        out_specs=(vmem,) * 3,
        scratch_shapes=[
            vm((128, 1280), bf16), vm((128, 1024), bf16), vm((64, 1280), f32), vm((64, 1024), f32),
            vm((1280, 1024), bf16), vm((32, 1280), bf16), vm((slots, 128), bf16), vm((slots, 128), bf16),
            vm((8, 128), bf16), vm((8, 128), bf16), pltpu.SMEM((8,), jnp.int32),
            vm((8, 8, 128), f32), vm((7, 8, 128), f32),
            vm((OWNERS, 8, 256), f32), vm((7, 8, 256), f32),
            vm((OWNERS, 8, 256), f32), vm((8, 256), f32), vm((8, 256), f32), vm((8, OWNERS, 8, 256), f32),
            vm((64, 8, 128), f32), vm((7, 8, 8, 128), f32), vm((8, 8, 8, 128), f32), vm((8, 8, 8, 128), f32),
            vm((4, 8, 1024), f32), vm((3, 8, 1024), f32),
            vm((8, 4, 1280), f32), vm((8, 4, 1280), f32),
            vm((8, 1, 128), f32), vm((64, 1, 128), f32), vm((1024, 64), bf16),
            dma((11,)), *two(7), *two(7), *two(1), *two(7), *two(32), *two(4),
            *two(7), *two(7), *two(7), *two(3), *two(8), dma, dma,
        ],
        compiler_params=pltpu.CompilerParams(
            collective_id=0, has_side_effects=True, vmem_limit_bytes=24 * 2**20
        ),
        name="exchange",
    )(*(pltpu.with_memory_space_constraint(v, pltpu.HBM) for v in arrays))
    at_new, b_new, attended = pl.pallas_call(
        finish,
        out_shape=outs,
        in_specs=[vmem] * 3,
        out_specs=(hbm,) * 3,
        scratch_shapes=[dma((3,))],
        compiler_params=pltpu.CompilerParams(vmem_limit_bytes=24 * 2**20),
        name="finish",
    )(*new)
    return at_new.T, b_new, attended


def solution(mesh):
    return jax.shard_map(
        local,
        mesh=mesh,
        in_specs=(
            P("group", "blk"),
            P("group", "tensor"),
            P("blk", None),
            P(None, "tensor"),
            P("blk", "tensor"),
            P("group", "blk"),
            P(("group", "blk"), None, "tensor"),
            P(("group", "blk"), None, "tensor"),
            P(("group", "blk"), "tensor"),
            P(("group", "blk"), "tensor"),
            P(("group", "blk")),
        ),
        out_specs=(P("blk", None), P(None, "tensor"), P(("group", "blk"), "tensor")),
        check_vma=False,
    )
```

time: 303 us -> 40.4 us (0.13)
  waiting for transfers between devices: 223 us -> 0 us
  blocking collectives: 42.8 us -> 0 us
  Pallas kernels: 0 us -> 39.6 us
  matrix products: 16.8 us -> 0 us
  between operations: 14.2 us -> 0.64 us
  other arithmetic: 3.35 us -> 0 us
    psum x1 -> x0, waiting for transfers between devices: 193 us -> none  [local(): group_down_gradient, group_up_gradient = lax.psum((part_a, part_b), 'group')]
    psum x2 -> x0, blocking collectives: 42.8 us -> none  [the longest x1 27.9 us: local(): lax.psum(jnp.dot(cotangent_rows, up_factor.T, precision=highest_precision...]
    pallas_call x0 -> x2, Pallas kernels: none -> 39.6 us  [the longest x1 38.8 us: local(): pl.pallas_call(exchange, out_shape=outs, in_specs=[hbm] * 11, out_specs=(...]
    reduce_scatter x1 -> x0, waiting for transfers between devices: 30.5 us -> none  [local(): lax.psum_scatter(jnp.dot(hidden_rows, merged, precision=highest_precision...]
    dot_general x9 -> x0, matrix products: 16.8 us -> none  [the longest x1 4.37 us: local(): jnp.dot(updated_down_factor, updated_up_factor, precision=highest_precision)]
  transfers between devices with their start and end apart: 2 -> 0, of which waited for: 2 -> 0; matrix products, arithmetic and copies ran while one was open for 0% -> 0% of each run, Pallas kernels for 0% -> 0%
where the time goes in v1:
time: 40.4 us; the launch traced here: 40.3 us
  Pallas kernels  39.6 us (98%)
  between operations  0.64 us (2%)
    pallas_call x1, Pallas kernels, local(): pl.pallas_call(exchange, out_shape=outs, in_specs=[hbm] * 11, out_specs=(...  38.8 us
    pallas_call x1, Pallas kernels, local(): pl.pallas_call(finish, out_shape=outs, in_specs=[vmem] * 3, out_specs=(hb...  0.84 us

profile of v1, /device:TPU:1, one launch (start us, length us, event | category | flops | bytes accessed | tf_op | source)
XLA Modules:
  0.0 40.3 jit_solution(17369196018274724595)
XLA Ops:
  0.6 38.8 %exchange.1 = (f32[64,1280]{1,0:T(8,128)S(1)}, f32[64,1024]{1,0:T(8,128)S(1)}, bf16[8,1024]{1,0:T(8,128)(2,1)S(1)}) custom-call(bf16[128,1280]{1,0:T(8,128)(2,1)} %x_any.1, bf16[128,1024]{1,0:T(8,128)(2,1)} %c_any.1, f32[64,1280]{1,0:T(8,128)} %bitcast.4, f32[64,1024]{1,0:T(8,128)} %b_any.1, bf16[1280,1024]{1,0:T(8,128)(2,1)} %w_any.1, ...), custom_call_target="tpu_custom_call" | custom-call | tf_op jit(solution)/shard_map/exchange/pallas_call | solution.py:343
  39.5 0.8 %finish.1 = (f32[64,1280]{1,0:T(8,128)}, f32[64,1024]{1,0:T(8,128)}, bf16[8,1024]{1,0:T(8,128)(2,1)}) custom-call(f32[64,1280]{1,0:T(8,128)S(1)} %get-tuple-element.9.at_in, f32[64,1024]{1,0:T(8,128)S(1)} %get-tuple-element.10.b_in, bf16[8,1024]{1,0:T(8,128)(2,1)S(1)} %get-tuple-element.11.att_in), custom_call_target="tpu_custom_call" | custom-call | tf_op jit(solution)/shard_map/finish/pallas_call | solution.py:367

commit v2 on v1

--- a/solution.py
+++ b/solution.py
@@ -16,6 +16,7 @@
 STEP = learning_rate * adapter_scale / TOKENS
 OWNERS = 5
 FAR_FIRST = (4, 5, 3, 7, 6, 2, 1)
+STAGES = ("p", "b1", "hx", "hx2", "a1", "a2", "a3", "b2", "hw", "a40", "a42", "a44", "a46", "u", "b3", "a5")
 
 
 def split(v):
@@ -45,8 +46,7 @@
     p_part, p_recv, a_part, a1_recv, a_half, a2_send, a2_recv, a_full,
     b_part, b1_recv, b_line, b_full,
     hw_part, hw_recv, hx_send, hx_recv, u_send, u_all, fold,
-    in_sem, p_s, p_r, a1_s, a1_r, a2_s, a2_r, a3_s, a3_r, a4_s, a4_r, a5_s, a5_r,
-    b1_s, b1_r, b2_s, b2_r, b3_s, b3_r, hw_s, hw_r, hx_s, hx_r, u_s, u_r,
+    in_sem, sems,
 ):
     g, t, b = lax.axis_index("group"), lax.axis_index("tensor"), lax.axis_index("blk")
     zh, y = lax.div(g, 8), lax.rem(g, 8)
@@ -94,29 +94,25 @@
     for copy in loads:
         copy.start()
 
-    arrivals, departures = {}, []
-
-    def send(name, src, dst, sems, i, device):
-        copy = pltpu.make_async_remote_copy(
-            src_ref=src, dst_ref=dst, send_sem=sems[0].at[i], recv_sem=sems[1].at[i],
+    def leaves(stage):
+        return sems.at[2 * STAGES.index(stage)]
+
+    def comes(stage):
+        return sems.at[2 * STAGES.index(stage) + 1]
+
+    def send(stage, src, dst, device):
+        pltpu.make_async_remote_copy(
+            src_ref=src, dst_ref=dst, send_sem=leaves(stage), recv_sem=comes(stage),
             device_id=device, device_id_type=MESH,
-        )
-        copy.start()
-        arrivals.setdefault(name, []).append(copy.wait_recv)
-        departures.append(copy.wait_send)
-
-    def send_if(name, out, src, come, dst, sems, i, device):
-        copy = pltpu.make_async_remote_copy(
-            src_ref=src, dst_ref=dst, send_sem=sems[0].at[i], recv_sem=sems[1].at[i],
-            device_id=device, device_id_type=MESH,
-        )
-        pl.when(out)(copy.start)
-        arrivals.setdefault(name, []).append(lambda: pl.when(come)(copy.wait_recv))
-        departures.append(lambda: pl.when(out)(copy.wait_send))
-
-    def arrive(name):
-        for wait in arrivals.pop(name):
-            wait()
+        ).start()
+
+    def wait(sem, ref):
+        pltpu.make_async_copy(ref, ref, sem).wait()
+
+    def wait_if(case, sem, ref, otherwise):
+        pl.when(case)(lambda: wait(sem, ref))
+        if otherwise is not None:
+            pl.when(jnp.logical_not(case))(lambda: wait(sem, otherwise))
 
     def rows(d):
         return pl.ds(pl.multiple_of(d * 8, 8), 8)
@@ -142,11 +138,11 @@
 
     pl.semaphore_wait(barrier, 21)
     for d in FAR_FIRST:
-        send("p", p_part.at[t ^ d], p_recv.at[d - 1], (p_s, p_r), d - 1, at_t(d))
-    for d in FAR_FIRST:
-        send("b1", b_part.at[rows(m ^ d)], b1_recv.at[d - 1], (b1_s, b1_r), d - 1, first(d))
-
-    send("hx", hx_send.at[t], hx_recv.at[t], (hx_s, hx_r), 0, at_z(4))
+        send("p", p_part.at[t ^ d], p_recv.at[d - 1], at_t(d))
+    for d in FAR_FIRST:
+        send("b1", b_part.at[rows(m ^ d)], b1_recv.at[d - 1], first(d))
+
+    send("hx", hx_send.at[t], hx_recv.at[t], at_z(4))
 
     into = lax.broadcasted_iota(jnp.int32, (1024, 64), 0)
     out = lax.broadcasted_iota(jnp.int32, (1024, 64), 1)
@@ -157,7 +153,7 @@
     hidden_chunk(0)
     hidden_chunk(1)
 
-    arrive("p")
+    wait(comes("p"), p_recv)
     back = p_part[t]
     for d in range(7):
         back = back + p_recv[d]
@@ -167,7 +163,8 @@
     owner = y < OWNERS
     piece = jnp.minimum(y, OWNERS - 1)
     for d in FAR_FIRST:
-        send_if("a1", (y ^ d) < OWNERS, a_part.at[jnp.minimum(y ^ d, OWNERS - 1)], owner, a1_recv.at[d - 1], (a1_s, a1_r), d - 1, at_y(d))
+        far = jnp.minimum(y ^ d, OWNERS - 1)
+        pl.when((y ^ d) < OWNERS)(lambda d=d, far=far: send("a1", a_part.at[far], a1_recv.at[d - 1], at_y(d)))
     hidden_chunk(2)
     hidden_chunk(3)
 
@@ -175,48 +172,43 @@
 
     @pl.when(owner)
     def _():
-        for wait in arrivals["a1"]:
-            wait()
+        wait(comes("a1"), a1_recv)
         total = a_part[piece]
         for d in range(7):
             total = total + a1_recv[d]
         a2_send[...] = total
         a_half[piece] = jnp.where(zh == 0, old, 0.0) - STEP * total
-
-    arrivals.pop("a1")
-    for d in FAR_FIRST:
-        send_if("a3", owner, a_half.at[piece], (y ^ d) < OWNERS, a_half.at[piece], (a3_s, a3_r), d - 1, at_y(d))
-    send_if("a2", owner, a2_send, owner, a2_recv, (a2_s, a2_r), 0, at_z(4))
-    arrive("hx")
-    for d in FAR_FIRST:
-        send("hx2", hx_recv.at[t], hx_recv.at[t], (hx_s, hx_r), d, at_t(d))
-
-    arrive("b1")
+        for d in FAR_FIRST:
+            send("a3", a_half.at[piece], a_half.at[piece], at_y(d))
+        send("a2", a2_send, a2_recv, at_z(4))
+
+
+    wait(comes("hx"), hx_recv.at[t])
+    for d in FAR_FIRST:
+        send("hx2", hx_recv.at[t], hx_recv.at[t], at_t(d))
+
+    wait(comes("b1"), b1_recv)
     total = b_part[rows(m)]
     for d in range(7):
         total = total + b1_recv[d]
     b_line[n] = total
     for d in FAR_FIRST:
-        send("b2", b_line.at[n], b_line.at[n], (b2_s, b2_r), d - 1, second(d))
+        send("b2", b_line.at[n], b_line.at[n], second(d))
     for d in (3, 2, 1):
-        send("hw", hw_part.at[b ^ d], hw_recv.at[d - 1], (hw_s, hw_r), d - 1, at_z(d))
+        send("hw", hw_part.at[b ^ d], hw_recv.at[d - 1], at_z(d))
 
     @pl.when(owner)
     def _():
-        for wait in arrivals["a2"]:
-            wait()
+        wait(comes("a2"), a2_recv)
         a_full[t, piece] = old - STEP * (a2_send[...] + a2_recv[...])
-
-    arrivals.pop("a2")
-    for i, dt in enumerate((4, 2, 6, 0)):
-        for d in FAR_FIRST + (0,):
-            if d or dt:
-                send_if(
-                    "a4" + str(dt), owner, a_full.at[t, piece], (y ^ d) < OWNERS, a_full.at[t, piece], (a4_s, a4_r), i * 8 + d, at_yt(d, dt)
-                )
-
-    arrive("a3")
-    arrive("hx2")
+        for dt in (4, 2, 6, 0):
+            for d in FAR_FIRST + (0,):
+                if d or dt:
+                    send("a4" + str(dt), a_full.at[t, piece], a_full.at[t, piece], at_yt(d, dt))
+
+
+    wait_if(owner, comes("a3"), a_half.at[pl.ds(0, OWNERS - 1)], a_half)
+    wait(comes("hx2"), hx_recv.at[pl.ds(0, 7)])
     near = jnp.zeros((64, 128), f32)
     both = jnp.concatenate([hid[...], hx_recv[...].reshape(32, 1280).astype(bf16)], axis=0)
     for i in range(OWNERS):
@@ -233,12 +225,12 @@
         for dt in (4, 5, 2, 3, 6, 7, 1, 0):
             if dz or dt:
                 copy = pltpu.make_async_remote_copy(
-                    src_ref=u_send.at[z ^ dz], dst_ref=u_all.at[t * 8 + z], send_sem=u_s, recv_sem=u_r,
+                    src_ref=u_send.at[z ^ dz], dst_ref=u_all.at[t * 8 + z], send_sem=leaves("u"), recv_sem=comes("u"),
                     device_id=at_zt(dz, dt), device_id_type=MESH,
                 )
                 copy.start()
 
-    arrive("b2")
+    wait(comes("b2"), b_line.at[pl.ds(0, 7)])
     total = b_line[0]
     for i in range(1, 8):
         total = total + b_line[i]
@@ -247,19 +239,22 @@
         tile = bu[rows(line), pl.ds(pl.multiple_of(col * 128, 128), 128)]
         b_full[m, i] = tile - STEP * total[i]
     for d in FAR_FIRST:
-        send("b3", b_full.at[m], b_full.at[m], (b3_s, b3_r), d - 1, first(d))
-
-    arrive("hw")
+        send("b3", b_full.at[m], b_full.at[m], first(d))
+
+    for i, dt in enumerate((0, 6, 2, 4)):
+        if dt:
+            wait(comes("a4" + str(dt)), a_full.at[t ^ dt])
+        else:
+            wait_if(owner, comes("a40"), a_full.at[t, pl.ds(0, OWNERS - 1)], a_full.at[t])
+        send("a5", a_full.at[t ^ dt], a_full.at[t ^ dt], at_t(1))
+
+    wait(comes("hw"), hw_recv)
     base = hw_part[b]
     for d in range(3):
         base = base + hw_recv[d]
 
-    for i, dt in enumerate((0, 6, 2, 4)):
-        arrive("a4" + str(dt))
-        send("a5", a_full.at[t ^ dt], a_full.at[t ^ dt], (a5_s, a5_r), i, at_t(1))
-
     most = u_all.at[pl.ds(0, 63)]
-    pltpu.make_async_copy(most, most, u_r).wait()
+    wait(comes("u"), most)
     slices = jnp.sum(u_all[...].reshape(8, 8, 1, 128), axis=1)
     lane = lax.broadcasted_iota(jnp.int32, (8, 128), 1)
     row = lax.broadcasted_iota(jnp.int32, (8, 128), 0)
@@ -268,7 +263,7 @@
     )
     hidden_low = twice(dot_nn, wide, fold[...])
 
-    arrive("b3")
+    wait(comes("b3"), b_full.at[pl.ds(0, 7)])
     for i in range(8):
         for j in range(8):
             first_at, second_at = jnp.where(y_first, j, i), jnp.where(y_first, i, j)
@@ -304,14 +299,26 @@
     for i in range(8):
         att_out[:, i * 128 : i * 128 + 128] = mixed[i]
 
-    arrive("a5")
+    wait(comes("a5"), a_full.at[pl.ds(0, 4)])
     for i in range(8):
         for j in range(OWNERS):
             at_out[i * 8 : i * 8 + 8, j * 256 : j * 256 + 256] = a_full[i, j]
 
-    for wait in departures:
-        wait()
-    pltpu.make_async_copy(most, most, u_s).wait()
+    for stage, ref in (
+        ("p", p_recv), ("b1", b1_recv), ("hx", hx_recv.at[t]), ("hx2", hx_recv.at[pl.ds(0, 7)]),
+        ("b2", b_line.at[pl.ds(0, 7)]), ("hw", hw_recv), ("u", most), ("b3", b_full.at[pl.ds(0, 7)]),
+        ("a5", a_full.at[pl.ds(0, 4)]),
+    ):
+        wait(leaves(stage), ref)
+    wait_if(owner, leaves("a1"), a_part.at[pl.ds(0, OWNERS - 1)], a_part)
+
+    @pl.when(owner)
+    def _():
+        wait(leaves("a3"), a1_recv)
+        wait(leaves("a2"), a2_recv)
+        wait(leaves("a40"), a1_recv)
+        for dt in (2, 4, 6):
+            wait(leaves("a4" + str(dt)), b_line.at[pl.ds(0, 2)])
 
 
 def finish(at_in, b_in, att_in, at_out, b_out, att_out, sem):
@@ -330,9 +337,6 @@
     slots = keys.shape[0] * keys.shape[1]
     hbm = pl.BlockSpec(memory_space=pltpu.HBM)
     vmem = pl.BlockSpec(memory_space=pltpu.VMEM)
-
-    def two(i):
-        return [dma((i,)), dma((i,))]
 
     outs = (
         jax.ShapeDtypeStruct((64, 1280), f32),
@@ -356,8 +360,7 @@
             vm((4, 8, 1024), f32), vm((3, 8, 1024), f32),
             vm((8, 4, 1280), f32), vm((8, 4, 1280), f32),
             vm((8, 1, 128), f32), vm((64, 1, 128), f32), vm((1024, 64), bf16),
-            dma((11,)), *two(7), *two(7), *two(1), *two(7), *two(32), *two(4),
-            *two(7), *two(7), *two(7), *two(3), *two(8), dma, dma,
+            dma((11,)), dma((2 * len(STAGES),)),
         ],
         compiler_params=pltpu.CompilerParams(
             collective_id=0, has_side_effects=True, vmem_limit_bytes=24 * 2**20

time: 40.4 us -> 39 us (0.965)
  Pallas kernels: 39.6 us -> 38.3 us
    pallas_call x1, Pallas kernels: 38.8 us -> 37.4 us  [local(): pl.pallas_call(exchange, out_shape=outs, in_specs=[hbm] * 11, out_specs=(...]
where the time goes in v2:
time: 39 us; the launch traced here: 38.9 us
  Pallas kernels  38.3 us (98%)
  between operations  0.64 us (2%)
    pallas_call x1, Pallas kernels, local(): pl.pallas_call(exchange, out_shape=outs, in_specs=[hbm] * 11, out_specs=(...  37.4 us
    pallas_call x1, Pallas kernels, local(): pl.pallas_call(finish, out_shape=outs, in_specs=[vmem] * 3, out_specs=(hb...  0.84 us

profile of v2, /device:TPU:1, one launch (start us, length us, event | category | flops | bytes accessed | tf_op | source)
XLA Modules:
  0.0 38.9 jit_solution(4366322258171720520)
XLA Ops:
  0.6 37.4 %exchange.1 = (f32[64,1280]{1,0:T(8,128)S(1)}, f32[64,1024]{1,0:T(8,128)S(1)}, bf16[8,1024]{1,0:T(8,128)(2,1)S(1)}) custom-call(bf16[128,1280]{1,0:T(8,128)(2,1)} %x_any.1, bf16[128,1024]{1,0:T(8,128)(2,1)} %c_any.1, f32[64,1280]{1,0:T(8,128)} %bitcast.4, f32[64,1024]{1,0:T(8,128)} %b_any.1, bf16[1280,1024]{1,0:T(8,128)(2,1)} %w_any.1, ...), custom_call_target="tpu_custom_call" | custom-call | tf_op jit(solution)/shard_map/exchange/pallas_call | solution.py:347
  38.1 0.8 %finish.1 = (f32[64,1280]{1,0:T(8,128)}, f32[64,1024]{1,0:T(8,128)}, bf16[8,1024]{1,0:T(8,128)(2,1)}) custom-call(f32[64,1280]{1,0:T(8,128)S(1)} %get-tuple-element.9.at_in, f32[64,1024]{1,0:T(8,128)S(1)} %get-tuple-element.10.b_in, bf16[8,1024]{1,0:T(8,128)(2,1)S(1)} %get-tuple-element.11.att_in), custom_call_target="tpu_custom_call" | custom-call | tf_op jit(solution)/shard_map/finish/pallas_call | solution.py:370

commit v3 on v2

--- a/solution.py
+++ b/solution.py
@@ -15,6 +15,7 @@
 TOKENS = 2048
 STEP = learning_rate * adapter_scale / TOKENS
 OWNERS = 5
+SHIFT = 2
 FAR_FIRST = (4, 5, 3, 7, 6, 2, 1)
 STAGES = ("p", "b1", "hx", "hx2", "a1", "a2", "a3", "b2", "hw", "a40", "a42", "a44", "a46", "u", "b3", "a5")
 
@@ -43,7 +44,7 @@
     x_any, c_any, at_any, b_any, w_any, h_any, k_any, v_any, ik_any, iv_any, len_any,
     at_out, b_out, att_out,
     x, c, at, bu, w, hid, kc, vc, ik, iv, lens,
-    p_part, p_recv, a_part, a1_recv, a_half, a2_send, a2_recv, a_full,
+    p_part, p_recv, a_part, a1_recv, a_half, a2_send, a2_recv,
     b_part, b1_recv, b_line, b_full,
     hw_part, hw_recv, hx_send, hx_recv, u_send, u_all, fold,
     in_sem, sems,
@@ -117,6 +118,9 @@
     def rows(d):
         return pl.ds(pl.multiple_of(d * 8, 8), 8)
 
+    def new_a(ranks, i):
+        return at_out.at[rows(ranks), pl.ds(pl.multiple_of(i * 256, 256), 256)]
+
     def hidden_chunk(i):
         cols = pl.ds(i * 256, 256)
         hw_part[:, :, cols] = dot_nn(hid[...], w[:, cols]).reshape(4, 8, 256)
@@ -160,11 +164,15 @@
     grad_a = twice(dot_nn, back, x[...])
     for i in range(OWNERS):
         a_part[i] = grad_a[:, i * 256 : i * 256 + 256]
-    owner = y < OWNERS
-    piece = jnp.minimum(y, OWNERS - 1)
-    for d in FAR_FIRST:
-        far = jnp.minimum(y ^ d, OWNERS - 1)
-        pl.when((y ^ d) < OWNERS)(lambda d=d, far=far: send("a1", a_part.at[far], a1_recv.at[d - 1], at_y(d)))
+
+    def piece_of(place):
+        return lax.rem(place + SHIFT, 8)
+
+    owner = piece_of(y) < OWNERS
+    piece = jnp.minimum(piece_of(y), OWNERS - 1)
+    for d in FAR_FIRST:
+        far = jnp.minimum(piece_of(y ^ d), OWNERS - 1)
+        pl.when(piece_of(y ^ d) < OWNERS)(lambda d=d, far=far: send("a1", a_part.at[far], a1_recv.at[d - 1], at_y(d)))
     hidden_chunk(2)
     hidden_chunk(3)
 
@@ -182,7 +190,6 @@
             send("a3", a_half.at[piece], a_half.at[piece], at_y(d))
         send("a2", a2_send, a2_recv, at_z(4))
 
-
     wait(comes("hx"), hx_recv.at[t])
     for d in FAR_FIRST:
         send("hx2", hx_recv.at[t], hx_recv.at[t], at_t(d))
@@ -200,17 +207,16 @@
     @pl.when(owner)
     def _():
         wait(comes("a2"), a2_recv)
-        a_full[t, piece] = old - STEP * (a2_send[...] + a2_recv[...])
+        at_out[rows(t), pl.ds(pl.multiple_of(piece * 256, 256), 256)] = old - STEP * (a2_send[...] + a2_recv[...])
         for dt in (4, 2, 6, 0):
             for d in FAR_FIRST + (0,):
                 if d or dt:
-                    send("a4" + str(dt), a_full.at[t, piece], a_full.at[t, piece], at_yt(d, dt))
-
-
+                    send("a4" + str(dt), new_a(t, piece), new_a(t, piece), at_yt(d, dt))
+
+    wait(comes("hx2"), hx_recv.at[pl.ds(0, 7)])
+    both = jnp.concatenate([hid[...], hx_recv[...].reshape(32, 1280).astype(bf16)], axis=0)
     wait_if(owner, comes("a3"), a_half.at[pl.ds(0, OWNERS - 1)], a_half)
-    wait(comes("hx2"), hx_recv.at[pl.ds(0, 7)])
     near = jnp.zeros((64, 128), f32)
-    both = jnp.concatenate([hid[...], hx_recv[...].reshape(32, 1280).astype(bf16)], axis=0)
     for i in range(OWNERS):
         hi, lo = split(jnp.concatenate([a_half[i]] * 8, axis=0))
         near = near + dot_nt(both[:, i * 256 : i * 256 + 256], jnp.concatenate([hi, lo], axis=0))
@@ -243,15 +249,24 @@
 
     for i, dt in enumerate((0, 6, 2, 4)):
         if dt:
-            wait(comes("a4" + str(dt)), a_full.at[t ^ dt])
+            wait(comes("a4" + str(dt)), at_out.at[rows(t ^ dt)])
         else:
-            wait_if(owner, comes("a40"), a_full.at[t, pl.ds(0, OWNERS - 1)], a_full.at[t])
-        send("a5", a_full.at[t ^ dt], a_full.at[t ^ dt], at_t(1))
+            wait_if(owner, comes("a40"), at_out.at[pl.ds(0, 8), pl.ds(0, 1024)], at_out.at[rows(t)])
+        send("a5", at_out.at[rows(t ^ dt)], at_out.at[rows(t ^ dt)], at_t(1))
 
     wait(comes("hw"), hw_recv)
     base = hw_part[b]
     for d in range(3):
         base = base + hw_recv[d]
+
+    for copy in loads[6:]:
+        copy.wait()
+    row = lax.broadcasted_iota(jnp.int32, (8, 128), 0)
+    slot = lax.broadcasted_iota(jnp.int32, (8, 128), 1)
+    live = jnp.concatenate(
+        [jnp.where((row == i) & (slot < lens[i]), 1.0, 0.0) for i in range(8)], axis=1
+    )[None]
+    live = jnp.broadcast_to(live, (8, 8, 1024)) > 0.5
 
     most = u_all.at[pl.ds(0, 63)]
     wait(comes("u"), most)
@@ -274,17 +289,9 @@
     both = dot_nn(jnp.concatenate([hi, lo], axis=0), b_hi)
     query = base + adapter_scale * (both[:8] + both[8:] + dot_nn(hi, b_lo))
 
-    for copy in loads[6:]:
-        copy.wait()
     heads = jnp.concatenate([query[:, i * 128 : i * 128 + 128] for i in range(8)], axis=0).astype(bf16)
     scale = 1.0 / math.sqrt(128)
     scores = (dot_nt(heads, kc[...]) * scale).reshape(8, 8, 1024)
-    row = lax.broadcasted_iota(jnp.int32, (8, 128), 0)
-    slot = lax.broadcasted_iota(jnp.int32, (8, 128), 1)
-    live = jnp.concatenate(
-        [jnp.where((row == i) & (slot < lens[i]), 1.0, 0.0) for i in range(8)], axis=1
-    )[None]
-    live = jnp.broadcast_to(live, scores.shape) > 0.5
     scores = jnp.where(live, scores, -1e30)
     own_k = ik[...].astype(f32)[None]
     own = jnp.sum(heads.astype(f32).reshape(8, 8, 128) * own_k, axis=-1, keepdims=True) * scale
@@ -299,15 +306,12 @@
     for i in range(8):
         att_out[:, i * 128 : i * 128 + 128] = mixed[i]
 
-    wait(comes("a5"), a_full.at[pl.ds(0, 4)])
-    for i in range(8):
-        for j in range(OWNERS):
-            at_out[i * 8 : i * 8 + 8, j * 256 : j * 256 + 256] = a_full[i, j]
+    wait(comes("a5"), at_out.at[pl.ds(0, 32)])
 
     for stage, ref in (
         ("p", p_recv), ("b1", b1_recv), ("hx", hx_recv.at[t]), ("hx2", hx_recv.at[pl.ds(0, 7)]),
         ("b2", b_line.at[pl.ds(0, 7)]), ("hw", hw_recv), ("u", most), ("b3", b_full.at[pl.ds(0, 7)]),
-        ("a5", a_full.at[pl.ds(0, 4)]),
+        ("a5", at_out.at[pl.ds(0, 32)]),
     ):
         wait(leaves(stage), ref)
     wait_if(owner, leaves("a1"), a_part.at[pl.ds(0, OWNERS - 1)], a_part)
@@ -355,7 +359,7 @@
             vm((8, 128), bf16), vm((8, 128), bf16), pltpu.SMEM((8,), jnp.int32),
             vm((8, 8, 128), f32), vm((7, 8, 128), f32),
             vm((OWNERS, 8, 256), f32), vm((7, 8, 256), f32),
-            vm((OWNERS, 8, 256), f32), vm((8, 256), f32), vm((8, 256), f32), vm((8, OWNERS, 8, 256), f32),
+            vm((OWNERS, 8, 256), f32), vm((8, 256), f32), vm((8, 256), f32),
             vm((64, 8, 128), f32), vm((7, 8, 8, 128), f32), vm((8, 8, 8, 128), f32), vm((8, 8, 8, 128), f32),
             vm((4, 8, 1024), f32), vm((3, 8, 1024), f32),
             vm((8, 4, 1280), f32), vm((8, 4, 1280), f32),

time: 39 us -> 38.1 us (0.977)
  Pallas kernels: 38.3 us -> 37.4 us
    pallas_call x1, Pallas kernels: 37.4 us -> 36.5 us  [local(): pl.pallas_call(exchange, out_shape=outs, in_specs=[hbm] * 11, out_specs=(...]
where the time goes in v3:
time: 38.1 us; the launch traced here: 38 us
  Pallas kernels  37.4 us (98%)
  between operations  0.64 us (2%)
    pallas_call x1, Pallas kernels, local(): pl.pallas_call(exchange, out_shape=outs, in_specs=[hbm] * 11, out_specs=(...  36.5 us
    pallas_call x1, Pallas kernels, local(): pl.pallas_call(finish, out_shape=outs, in_specs=[vmem] * 3, out_specs=(hb...  0.84 us

profile of v3, /device:TPU:1, one launch (start us, length us, event | category | flops | bytes accessed | tf_op | source)
XLA Modules:
  0.0 38.0 jit_solution(6393041482213889630)
XLA Ops:
  0.6 36.5 %exchange.1 = (f32[64,1280]{1,0:T(8,128)S(1)}, f32[64,1024]{1,0:T(8,128)S(1)}, bf16[8,1024]{1,0:T(8,128)(2,1)S(1)}) custom-call(bf16[128,1280]{1,0:T(8,128)(2,1)} %x_any.1, bf16[128,1024]{1,0:T(8,128)(2,1)} %c_any.1, f32[64,1280]{1,0:T(8,128)} %bitcast.4, f32[64,1024]{1,0:T(8,128)} %b_any.1, bf16[1280,1024]{1,0:T(8,128)(2,1)} %w_any.1, ...), custom_call_target="tpu_custom_call" | custom-call | tf_op jit(solution)/shard_map/exchange/pallas_call | solution.py:351
  37.2 0.8 %finish.1 = (f32[64,1280]{1,0:T(8,128)}, f32[64,1024]{1,0:T(8,128)}, bf16[8,1024]{1,0:T(8,128)(2,1)}) custom-call(f32[64,1280]{1,0:T(8,128)S(1)} %get-tuple-element.9.at_in, f32[64,1024]{1,0:T(8,128)S(1)} %get-tuple-element.10.b_in, bf16[8,1024]{1,0:T(8,128)(2,1)S(1)} %get-tuple-element.11.att_in), custom_call_target="tpu_custom_call" | custom-call | tf_op jit(solution)/shard_map/finish/pallas_call | solution.py:374

commit v4 on v3

--- a/solution.py
+++ b/solution.py
@@ -154,8 +154,8 @@
     fold[...] = jnp.where(hit, 1.0, 0.0).astype(bf16)
 
     loads[5].wait()
-    hidden_chunk(0)
-    hidden_chunk(1)
+    for i in range(4):
+        hidden_chunk(i)
 
     wait(comes("p"), p_recv)
     back = p_part[t]
@@ -173,8 +173,6 @@
     for d in FAR_FIRST:
         far = jnp.minimum(piece_of(y ^ d), OWNERS - 1)
         pl.when(piece_of(y ^ d) < OWNERS)(lambda d=d, far=far: send("a1", a_part.at[far], a1_recv.at[d - 1], at_y(d)))
-    hidden_chunk(2)
-    hidden_chunk(3)
 
     old = at[rows(t), pl.ds(pl.multiple_of(piece * 256, 256), 256)]
 
@@ -208,7 +206,7 @@
     def _():
         wait(comes("a2"), a2_recv)
         at_out[rows(t), pl.ds(pl.multiple_of(piece * 256, 256), 256)] = old - STEP * (a2_send[...] + a2_recv[...])
-        for dt in (4, 2, 6, 0):
+        for dt in (0, 4, 2, 6):
             for d in FAR_FIRST + (0,):
                 if d or dt:
                     send("a4" + str(dt), new_a(t, piece), new_a(t, piece), at_yt(d, dt))
@@ -227,8 +225,8 @@
     u_send[pl.ds(zh * 4, 4)] = near[0]
     u_send[pl.ds(4 - zh * 4, 4)] = near[1]
     u_all[t * 8 + z] = u_send[z]
-    for dz in (4, 5, 3, 7, 6, 2, 1, 0):
-        for dt in (4, 5, 2, 3, 6, 7, 1, 0):
+    for dt in (4, 5, 2, 3, 6, 7, 1, 0):
+        for dz in (4, 5, 3, 7, 6, 2, 1, 0):
             if dz or dt:
                 copy = pltpu.make_async_remote_copy(
                     src_ref=u_send.at[z ^ dz], dst_ref=u_all.at[t * 8 + z], send_sem=leaves("u"), recv_sem=comes("u"),

time: 38.1 us -> 38.1 us (level)
  no operation moved by 1% of the time
where the time goes in v4:
time: 38.1 us; the launch traced here: 38 us
  Pallas kernels  37.4 us (98%)
  between operations  0.64 us (2%)
    pallas_call x1, Pallas kernels, local(): pl.pallas_call(exchange, out_shape=outs, in_specs=[hbm] * 11, out_specs=(...  36.5 us
    pallas_call x1, Pallas kernels, local(): pl.pallas_call(finish, out_shape=outs, in_specs=[vmem] * 3, out_specs=(hb...  0.84 us

profile of v4, /device:TPU:1, one launch (start us, length us, event | category | flops | bytes accessed | tf_op | source)
XLA Modules:
  0.0 38.0 jit_solution(13827116192140739254)
XLA Ops:
  0.6 36.5 %exchange.1 = (f32[64,1280]{1,0:T(8,128)S(1)}, f32[64,1024]{1,0:T(8,128)S(1)}, bf16[8,1024]{1,0:T(8,128)(2,1)S(1)}) custom-call(bf16[128,1280]{1,0:T(8,128)(2,1)} %x_any.1, bf16[128,1024]{1,0:T(8,128)(2,1)} %c_any.1, f32[64,1280]{1,0:T(8,128)} %bitcast.4, f32[64,1024]{1,0:T(8,128)} %b_any.1, bf16[1280,1024]{1,0:T(8,128)(2,1)} %w_any.1, ...), custom_call_target="tpu_custom_call" | custom-call | tf_op jit(solution)/shard_map/exchange/pallas_call | solution.py:349
  37.2 0.8 %finish.1 = (f32[64,1280]{1,0:T(8,128)}, f32[64,1024]{1,0:T(8,128)}, bf16[8,1024]{1,0:T(8,128)(2,1)}) custom-call(f32[64,1280]{1,0:T(8,128)S(1)} %get-tuple-element.9.at_in, f32[64,1024]{1,0:T(8,128)S(1)} %get-tuple-element.10.b_in, bf16[8,1024]{1,0:T(8,128)(2,1)S(1)} %get-tuple-element.11.att_in), custom_call_target="tpu_custom_call" | custom-call | tf_op jit(solution)/shard_map/finish/pallas_call | solution.py:372
